TPU v7x, 32 devices: a whole 2x2x4 slice. The times are simulated.
32 devices in a mesh: tr: 4 (over x, core), gz: 8 (over z, y).
Axes of the slice: x: 2, y: 2, z: 4, core: 2. Of those that a mesh axis runs over, the one named last changes fastest.
Arguments:
- tokens: bfloat16 [40, 32, 8, 768], P('gz', None, 'tr'), may hold values from -6 to 6
- cotangent: bfloat16 [40, 32, 8, 768], P('gz', None, 'tr'), may hold values from -6 to 6
- gain_x: float32 [768], replicated, may hold values from 0.1 to 1.9
- wqkv_x: bfloat16 [768, 2304], P('tr'), as said below
- wo_x: bfloat16 [768, 768], P('tr'), may hold values from -0.21875 to 0.21875
- gain_z: float32 [768], replicated, may hold values from 0.1 to 1.9
- wqkv_z: bfloat16 [768, 2304], P('tr'), as said below
- wo_z: bfloat16 [768, 768], P('tr'), may hold values from -0.21875 to 0.21875
Outputs:
- grad_tokens: bfloat16 [40, 32, 8, 768], P('gz', None, 'tr')
Inputs may be any that keep to these rules, and one draw needn't show every extreme that they name: `wqkv_x`: query, key and value columns side by side, each block split into 6 heads of 128. `wqkv_z`: query, key and value columns side by side, each block split into 6 heads of 128.
All inputs are finite; a program needn't handle non-finite values.
Results may differ from a plain program's by a relative error of at most 0.038.
The roundings to bfloat16 on the way count: a program that leaves them out, or rounds other values in their place, can miss the bound.
Values may be sent and summed in bfloat16 or wider, within the bound.
A program may use at most 64 MiB of HBM per device.

v0:
```python
import math
import jax
import jax.numpy as jnp
from jax import lax
from jax.sharding import PartitionSpec as P

H = 6


def head_split(packed, index, model_width):
    piece = packed[..., index * model_width : (index + 1) * model_width]
    return piece.reshape(piece.shape[:-1] + (H, model_width // H))


def merge_heads(value):
    return value.reshape(value.shape[:-2] + (value.shape[-2] * value.shape[-1],))


def recompute(tokens_in, gain_vec, w_in, layout):
    model_width = w_in.shape[0]
    factor = 1.0 / math.sqrt(model_width // H)
    widened = tokens_in.astype(jnp.float32)
    inv_rms = lax.rsqrt(jnp.mean(widened * widened, axis=-1, keepdims=True) + 1e-06)
    normed = (widened * inv_rms * gain_vec).astype(jnp.bfloat16)
    packed = jnp.dot(normed, w_in, preferred_element_type=jnp.float32).astype(jnp.bfloat16)
    queries = head_split(packed, 0, model_width)
    key_part = head_split(packed, 1, model_width)
    values = head_split(packed, 2, model_width)
    key_form = layout.replace("l", "m")
    scores = (
        jnp.einsum(
            layout + "," + key_form + "->bhlm",
            queries,
            key_part,
            preferred_element_type=jnp.float32,
        )
        * factor
    )
    highest = jnp.max(scores, axis=-1, keepdims=True)
    expanded = jnp.exp(scores - highest)
    probs = expanded / jnp.sum(expanded, axis=-1, keepdims=True)
    return (widened, inv_rms, queries, key_part, values, probs, probs.astype(jnp.bfloat16), factor)


def forward_out(tokens_in, gain_vec, w_in, w_out, layout):
    widened, inv_rms, queries, key_part, values, probs, probs_b, factor = recompute(
        tokens_in, gain_vec, w_in, layout
    )
    key_form = layout.replace("l", "m")
    mixed = jnp.einsum(
        "bhlm," + key_form + "->" + layout, probs_b, values, preferred_element_type=jnp.float32
    )
    mixed = merge_heads(mixed.astype(jnp.bfloat16))
    return (widened + jnp.dot(mixed, w_out, preferred_element_type=jnp.float32)).astype(
        jnp.bfloat16
    )


def backward(tokens_in, upstream, gain_vec, w_in, w_out, layout):
    widened, inv_rms, queries, key_part, values, probs, probs_b, factor = recompute(
        tokens_in, gain_vec, w_in, layout
    )
    key_form = layout.replace("l", "m")
    d_mixed = jnp.dot(upstream, w_out.T, preferred_element_type=jnp.float32).astype(jnp.bfloat16)
    d_mixed = d_mixed.reshape(d_mixed.shape[:-1] + (H, d_mixed.shape[-1] // H))
    d_probs = jnp.einsum(
        layout + "," + key_form + "->bhlm", d_mixed, values, preferred_element_type=jnp.float32
    )
    d_values = jnp.einsum(
        "bhlm," + layout + "->" + key_form, probs_b, d_mixed, preferred_element_type=jnp.float32
    ).astype(jnp.bfloat16)
    centre = jnp.sum(probs * d_probs, axis=-1, keepdims=True)
    d_scores = (probs * (d_probs - centre) * factor).astype(jnp.bfloat16)
    d_queries = jnp.einsum(
        "bhlm," + key_form + "->" + layout, d_scores, key_part, preferred_element_type=jnp.float32
    ).astype(jnp.bfloat16)
    d_keys = jnp.einsum(
        "bhlm," + layout + "->" + key_form, d_scores, queries, preferred_element_type=jnp.float32
    ).astype(jnp.bfloat16)
    joined = jnp.concatenate(
        [merge_heads(d_queries), merge_heads(d_keys), merge_heads(d_values)], axis=-1
    )
    d_normed = jnp.dot(joined, w_in.T, preferred_element_type=jnp.float32)
    scaled = d_normed * gain_vec
    d_tokens = inv_rms * (
        scaled - widened * inv_rms * inv_rms * jnp.mean(scaled * widened, axis=-1, keepdims=True)
    )
    return (upstream.astype(jnp.float32) + d_tokens).astype(jnp.bfloat16)


def line_forward(lines, gain_vec, w_in, w_out):
    feature_count = lines.shape[3]
    flat = lines.reshape(-1, lines.shape[2], feature_count)
    return forward_out(flat, gain_vec, w_in, w_out, "blhe").reshape(lines.shape)


def line_backward(lines, upstream, gain_vec, w_in, w_out):
    feature_count = lines.shape[3]
    flat = lines.reshape(-1, lines.shape[2], feature_count)
    flat_up = upstream.reshape(flat.shape)
    return backward(flat, flat_up, gain_vec, w_in, w_out, "blhe").reshape(lines.shape)


def per_device(tokens, cotangent, gain_x, wqkv_x, wo_x, gain_z, wqkv_z, wo_z):
    full_in_x, full_out_x = (
        lax.all_gather(wqkv_x, "tr", axis=0, tiled=True),
        lax.all_gather(wo_x, "tr", axis=0, tiled=True),
    )
    full_in_z, full_out_z = (
        lax.all_gather(wqkv_z, "tr", axis=0, tiled=True),
        lax.all_gather(wo_z, "tr", axis=0, tiled=True),
    )
    width = tokens.shape[-1]
    lines = lax.all_to_all(tokens, "tr", split_axis=1, concat_axis=2, tiled=True)
    cot_lines = lax.all_to_all(cotangent, "tr", split_axis=1, concat_axis=2, tiled=True)
    cells = lines.shape[1] * lines.shape[2]
    flat = (lines.shape[0], cells, width)
    cot_columns = lax.all_to_all(
        cot_lines.reshape(flat), "gz", split_axis=1, concat_axis=0, tiled=True
    )
    mid_lines = line_forward(lines, gain_x, full_in_x, full_out_x)
    mid_columns = lax.all_to_all(
        mid_lines.reshape(flat), "gz", split_axis=1, concat_axis=0, tiled=True
    )
    grad_columns = backward(mid_columns, cot_columns, gain_z, full_in_z, full_out_z, "lbhe")
    grad_lines = lax.all_to_all(grad_columns, "gz", split_axis=0, concat_axis=1, tiled=True)
    result_lines = line_backward(
        lines, grad_lines.reshape(lines.shape), gain_x, full_in_x, full_out_x
    )
    return lax.all_to_all(result_lines, "tr", split_axis=2, concat_axis=1, tiled=True)


def solution(mesh):
    return jax.shard_map(
        per_device,
        mesh=mesh,
        in_specs=(
            P("gz", None, "tr", None),
            P("gz", None, "tr", None),
            P(),
            P("tr", None),
            P("tr", None),
            P(),
            P("tr", None),
            P("tr", None),
        ),
        out_specs=P("gz", None, "tr", None),
        check_vma=False,
    )
```

profile of v0, /device:TPU:0, one launch (start us, length us, event | category | flops | bytes accessed | tf_op | source)
XLA Modules:
  0.0 194.4 jit_solution(14103475853062895245)
XLA Ops:
  6.5 0.7 all-gather.5.cloned.1.call-update
  7.3 0.0 all-gather.7.cloned.1.call-start
  7.3 0.7 all-gather.7.cloned.1.call-update
  8.0 0.0 all-gather.11.cloned.1.call-start
  8.1 0.7 all-gather.11.cloned.1.call-update
  8.8 0.0 all-gather.9.cloned.1.call-start
  8.8 0.5 all-gather.9.cloned.1.call-update
  9.3 1.1 copy.114
  10.5 4.2 %all-to-all-start.2 = ((bf16[5,32,2,768]{3,2,0,1:T(2,128)(2,1)}), bf16[5,32,2,768]{3,2,0,1:T(2,128)(2,1)S(1)}, u32[]{:S(2)}, u32[]{:S(2)}) async-start(bf16[5,32,2,768]{3,2,0,1:T(2,128)(2,1)} %copy.114), calls=%async_computation.2 | async-start | bytes 983040 | tf_op jit(solution)/shard_map/all_to_all | solution.py:114
  14.7 1.1 copy.109
  15.8 9.2 %all-to-all-done.2 = bf16[5,32,2,768]{3,2,0,1:T(2,128)(2,1)S(1)} async-done(((bf16[5,32,2,768]{3,2,0,1:T(2,128)(2,1)}), bf16[5,32,2,768]{3,2,0,1:T(2,128)(2,1)S(1)}, u32[]{:S(2)}, u32[]{:S(2)}) %all-to-all-start.2) | async-done | bytes 491552 | tf_op jit(solution)/shard_map/all_to_all | solution.py:114
  25.0 3.5 %all-to-all-start = ((bf16[5,32,2,768]{3,2,0,1:T(2,128)(2,1)}), bf16[5,32,2,768]{3,2,0,1:T(2,128)(2,1)S(1)}, u32[]{:S(2)}, u32[]{:S(2)}) async-start(bf16[5,32,2,768]{3,2,0,1:T(2,128)(2,1)} %copy.109), calls=%async_computation | async-start | bytes 983040 | tf_op jit(solution)/shard_map/all_to_all | solution.py:115
  28.4 0.6 multiply_reduce_fusion.4
  29.1 0.2 copy.178
  29.3 0.1 rsqrt.24
  29.3 0.1 copy.119
  29.4 13.1 %all-to-all-done = bf16[5,32,2,768]{3,2,0,1:T(2,128)(2,1)S(1)} async-done(((bf16[5,32,2,768]{3,2,0,1:T(2,128)(2,1)}), bf16[5,32,2,768]{3,2,0,1:T(2,128)(2,1)S(1)}, u32[]{:S(2)}, u32[]{:S(2)}) %all-to-all-start) | async-done | bytes 491552 | tf_op jit(solution)/shard_map/all_to_all | solution.py:115
  42.5 1.0 copy.144
  43.5 7.3 %all-to-all-start.1 = ((bf16[5,64,768]{2,0,1:T(8,128)(2,1)}), bf16[5,64,768]{2,0,1:T(8,128)(2,1)S(1)}, u32[]{:S(2)}, u32[]{:S(2)}) async-start(bf16[5,64,768]{2,0,1:T(8,128)(2,1)} %bitcast.2), calls=%async_computation.1 | async-start | bytes 1572864 | tf_op jit(solution)/shard_map/all_to_all | solution.py:118
  50.8 0.4 copy_bitcast_fusion
  51.2 0.7 reshape.140
  51.9 0.0 all-gather.5.cloned.1.call-done
  51.9 3.4 %convolution_convert_fusion.1 = bf16[40,8,2304]{2,1,0:T(8,128)(2,1)S(1)} fusion(bf16[768,2304]{1,0:T(8,128)(2,1)} %all-gather.5.cloned.1.call-done, f32[40,8,768]{2,1,0:T(8,128)S(1)} %reshape.140, f32[768]{0:T(1024)S(1)} %copy-done.8, f32[40,8]{1,0:T(8,128)S(1)} %copy.119), kind=kOutput, calls=%fused_computation.5 | convolution fusion | flops 1133936640 | bytes 6000896 | tf_op jit(solution)/shard_map/dot_general | solution.py:25
  55.3 1.8 fusion.105
  57.1 11.9 %all-gather.7.cloned.1.call-done = bf16[768,768]{1,0:T(8,128)(2,1)} async-done(((bf16[192,768]{1,0:T(8,128)(2,1)}), bf16[768,768]{1,0:T(8,128)(2,1)}) %all-gather.7.cloned.1.call-update) | async-done | bytes 1179664 | tf_op jit(solution)/shard_map/all_gather | solution.py:107
  69.0 2.6 %fusion.40 = bf16[40,8,768]{2,1,0:T(8,128)(2,1)S(1)} fusion(f32[40,8,768]{2,1,0:T(8,128)S(1)} %reshape.140, bf16[768,768]{1,0:T(8,128)(2,1)} %all-gather.7.cloned.1.call-done, bf16[40,8,2304]{2,1,0:T(8,128)(2,1)} %copy-done.5, f32[40,6,8,8]{2,3,1,0:T(8,128)} %get-tuple-element.9, f32[40,6,8]{2,1,0:T(8,128)S(1)} %get-tuple-element.8), kind=kOutput, calls=%fused_computation.38 | convolution fusion | flops 382187520 | bytes 4136448 | tf_op jit(solution)/shard_map/dot_general | solution.py:54
  71.7 1.2 copy.121
  72.9 0.0 all-to-all-done.1
  72.9 5.5 %all-to-all-start.3 = ((bf16[5,64,768]{2,0,1:T(8,128)(2,1)}), bf16[5,64,768]{2,0,1:T(8,128)(2,1)S(1)}, u32[]{:S(2)}, u32[]{:S(2)}) async-start(bf16[5,64,768]{2,0,1:T(8,128)(2,1)} %copy.121), calls=%async_computation.3 | async-start | bytes 1572864 | tf_op jit(solution)/shard_map/all_to_all | solution.py:122
  78.4 0.1 copy.113
  78.5 9.5 %all-gather.11.cloned.1.call-done = bf16[768,768]{1,0:T(8,128)(2,1)} async-done(((bf16[192,768]{1,0:T(8,128)(2,1)}), bf16[768,768]{1,0:T(8,128)(2,1)}) %all-gather.11.cloned.1.call-update) | async-done | bytes 1179664 | tf_op jit(solution)/shard_map/all_gather | solution.py:111
  88.1 2.6 %fusion.43 = bf16[40,8,6,128]{3,1,2,0:T(8,128)(2,1)} fusion(bf16[40,8,768]{2,1,0:T(8,128)(2,1)S(1)} %bitcast.138, bf16[768,768]{1,0:T(8,128)(2,1)} %all-gather.11.cloned.1.call-done), kind=kOutput, calls=%fused_computation.50 | convolution fusion | flops 377733120 | bytes 2162688 | tf_op jit(solution)/shard_map/dot_general | solution.py:64
  90.7 8.3 %all-to-all-done.3 = bf16[5,64,768]{2,0,1:T(8,128)(2,1)S(1)} async-done(((bf16[5,64,768]{2,0,1:T(8,128)(2,1)}), bf16[5,64,768]{2,0,1:T(8,128)(2,1)S(1)}, u32[]{:S(2)}, u32[]{:S(2)}) %all-to-all-start.3) | async-done | bytes 491552 | tf_op jit(solution)/shard_map/all_to_all | solution.py:122
  99.0 0.3 multiply_reduce_fusion
  99.3 0.1 copy.122
  99.3 0.1 reshape.151
  99.5 0.1 copy.125
  99.6 20.7 %all-gather.9.cloned.1.call-done = bf16[768,2304]{1,0:T(8,128)(2,1)} async-done(((bf16[192,2304]{1,0:T(8,128)(2,1)}), bf16[768,2304]{1,0:T(8,128)(2,1)}) %all-gather.9.cloned.1.call-update) | async-done | bytes 3538960 | tf_op jit(solution)/shard_map/all_gather | solution.py:110
  120.3 3.3 %convolution_convert_fusion = bf16[40,8,2304]{2,1,0:T(8,128)(2,1)S(1)} fusion(bf16[768,2304]{1,0:T(8,128)(2,1)} %all-gather.9.cloned.1.call-done, f32[40,8,768]{2,1,0:T(8,128)S(1)} %bitcast.135, f32[768]{0:T(1024)S(1)} %copy-done.7, f32[40,8]{1,0:T(8,128)S(1)} %reshape.158), kind=kOutput, calls=%fused_computation.4 | convolution fusion | flops 1133936640 | bytes 6000896 | tf_op jit(solution)/shard_map/dot_general | solution.py:25
  123.7 0.0 copy-start.4
  123.7 0.9 slice_bitcast_fusion
  124.6 0.2 copy-done.4
  124.8 0.4 fusion.60
  125.2 2.6 %fusion.106 = (f32[8,6,40]{2,1,0:T(8,128)S(1)}, f32[8,6,40,40]{2,3,1,0:T(8,128)}) fusion(bf16[40,8,6,128]{3,1,2,0:T(8,128)(2,1)S(1)} %get-tuple-element.7, bf16[40,8,6,128]{3,1,2,0:T(8,128)(2,1)} %get-tuple-element.6), kind=kOutput, calls=%fused_computation.123 | convolution fusion | flops 19891240 | bytes 1297920 | tf_op jit(solution)/shard_map/sub | solution.py:40
  127.8 2.6 %fusion.48 = bf16[40,8,6,128]{3,0,2,1:T(8,128)(2,1)} fusion(bf16[40,8,6,128]{3,1,2,0:T(8,128)(2,1)} %fusion.43, f32[8,6,40,40]{2,3,1,0:T(8,128)} %get-tuple-element.11, f32[8,6,40]{2,1,0:T(8,128)S(1)} %get-tuple-element.10), kind=kOutput, calls=%fused_computation.55 | convolution fusion | flops 20060160 | bytes 1297920 | tf_op jit(solution)/shard_map/bhlm,lbhe->mbhe/dot_general | solution.py:69
  130.3 3.0 %fusion.47 = bf16[40,8,6,128]{3,0,2,1:T(8,128)(2,1)} fusion(f32[8,6,40,40]{2,3,1,0:T(8,128)S(1)} %fusion.60, bf16[40,8,6,128]{3,1,2,0:T(8,128)(2,1)} %get-tuple-element.6, f32[8,6,40,40]{2,3,1,0:T(8,128)} %get-tuple-element.11, f32[8,6,40]{2,1,0:T(8,128)S(1)} %get-tuple-element.10), kind=kOutput, calls=%fused_computation.54 | convolution fusion | flops 20446120 | bytes 1605120 | tf_op jit(solution)/shard_map/bhlm,lbhe->mbhe/dot_general | solution.py:77
  133.3 2.9 %fusion.46 = bf16[40,8,6,128]{3,0,2,1:T(8,128)(2,1)} fusion(f32[8,6,40,40]{2,3,1,0:T(8,128)S(1)} %fusion.60, bf16[40,8,6,128]{3,1,2,0:T(8,128)(2,1)S(1)} %get-tuple-element.7, f32[8,6,40,40]{2,3,1,0:T(8,128)} %get-tuple-element.11, f32[8,6,40]{2,1,0:T(8,128)S(1)} %get-tuple-element.10), kind=kOutput, calls=%fused_computation.53 | convolution fusion | flops 20446120 | bytes 1605120 | tf_op jit(solution)/shard_map/bhlm,mbhe->lbhe/dot_general | solution.py:74
  136.3 1.2 copy.183
  137.4 1.4 copy_bitcast_fusion.1
  138.8 3.5 %multiply_reduce_fusion.3 = (f32[40,8]{1,0:T(8,128)S(1)}, f32[40,8,768]{2,1,0:T(8,128)S(1)}) fusion(f32[40,8,768]{2,1,0:T(8,128)S(1)} %bitcast.136, f32[768]{0:T(1024)S(1)} %copy-done.7, bf16[768,2304]{1,0:T(8,128)(2,1)} %all-gather.9.cloned.1.call-done, bf16[40,8,768]{2,1,0:T(8,128)(2,1)S(1)} %get-tuple-element.16, ...), kind=kOutput, calls=%fused_computation.69 | convolution fusion | flops 1137622784 | bytes 6983936 | tf_op jit(solution)/shard_map/dot_general | solution.py:83
  142.3 0.3 add_convert_fusion.1
  142.6 19.6 %all_to_all.84 = bf16[40,8,768]{2,1,0:T(8,128)(2,1)S(1)} all-to-all(bf16[40,8,768]{2,1,0:T(8,128)(2,1)S(1)} %add_convert_fusion.1), channel_id=1, replica_groups=mesh['tr'=4,'gz'=8] {'gz'}, dimensions={0} | all-to-all | bytes 983040 | tf_op jit(solution)/shard_map/all_to_all | solution.py:126
  162.3 0.6 fusion.44
  162.9 0.6 copy-done.9
  163.5 0.0 copy-done.12
  163.5 1.2 fusion.51
  164.7 1.5 fusion.79
  166.2 2.7 %fusion.49 = bf16[40,8,768]{2,1,0:T(8,128)(2,1)} fusion(f32[40,6,8,8]{2,3,1,0:T(8,128)S(1)} %fusion.79, bf16[40,8,2304]{2,1,0:T(8,128)(2,1)} %copy-done.5, f32[40,6,8,8]{2,3,1,0:T(8,128)S(1)} %copy-done.10, f32[40,6,8]{2,1,0:T(8,128)} %copy-done.11), kind=kOutput, calls=%fused_computation.56 | convolution fusion | flops 4287367 | bytes 5242880 | tf_op jit(solution)/shard_map/bhlm,bmhe->blhe/dot_general | solution.py:74
  168.9 2.6 %fusion.50 = bf16[40,8,768]{2,1,0:T(8,128)(2,1)} fusion(f32[40,6,8,8]{2,3,1,0:T(8,128)S(1)} %fusion.79, bf16[40,8,2304]{2,1,0:T(8,128)(2,1)} %copy-done.5, f32[40,6,8,8]{2,3,1,0:T(8,128)S(1)} %copy-done.10, f32[40,6,8]{2,1,0:T(8,128)} %copy-done.11), kind=kOutput, calls=%fused_computation.57 | convolution fusion | flops 4287367 | bytes 5242880 | tf_op jit(solution)/shard_map/bhlm,blhe->bmhe/dot_general | solution.py:77
  171.5 3.9 %multiply_reduce_fusion.2 = (f32[40,8]{1,0:T(8,128)S(1)}, f32[40,8,768]{2,1,0:T(8,128)S(1)}) fusion(f32[40,8,768]{2,1,0:T(8,128)S(1)} %reshape.140, f32[768]{0:T(1024)S(1)} %copy-done.8, bf16[768,2304]{1,0:T(8,128)(2,1)} %all-gather.5.cloned.1.call-done, bf16[40,8,768]{2,1,0:T(8,128)(2,1)} %fusion.51, bf16[40,8,768]{2,1,0:T(8,128)(2,1)} %fusion.50, ...), kind=kOutput, calls=%fused_computation.67 | convolution fusion | flops 1137622784 | bytes 6983936 | tf_op jit(solution)/shard_map/dot_general | solution.py:83
  175.4 0.3 add_convert_fusion
  175.8 0.1 copy.139
  175.9 10.9 %all_to_all.85 = bf16[5,8,8,768]{3,1,0,2:T(8,128)(2,1)S(1)} all-to-all(bf16[5,8,8,768]{3,1,0,2:T(8,128)(2,1)S(1)} %copy.139), channel_id=1, replica_groups=mesh['tr'=4,'gz'=8] {'tr'}, dimensions={2} | all-to-all | bytes 983040 | tf_op jit(solution)/shard_map/all_to_all | solution.py:130
  186.7 1.2 copy.140
  (31 shorter events, 0.2 us)
Async XLA Ops:
  6.5 2.8 %copy-start.2 = (bf16[5,32,2,768]{3,2,1,0:T(2,128)(2,1)S(1)}, bf16[5,32,2,768]{3,2,1,0:T(2,128)(2,1)}, u32[]{:S(2)}) copy-start(bf16[5,32,2,768]{3,2,1,0:T(2,128)(2,1)} %param.8) | copy-start | bytes 1474564
  6.5 45.4 %all-gather.5.cloned.1.call-start = ((), (), s32[]{:S(2)}) async-start(), calls=%async_computation.6 | async-start | bytes 4423680 | tf_op jit(solution)/shard_map/all_gather | solution.py:106
  7.3 61.8 %all-gather.7.cloned.1.call-start = ((), (), s32[]{:S(2)}) async-start(), calls=%async_computation.7 | async-start | bytes 1474560 | tf_op jit(solution)/shard_map/all_gather | solution.py:107
  8.0 80.1 %all-gather.11.cloned.1.call-start = ((), (), s32[]{:S(2)}) async-start(), calls=%async_computation.9 | async-start | bytes 1474560 | tf_op jit(solution)/shard_map/all_gather | solution.py:111
  8.7 5.9 %copy-start.3 = (bf16[5,32,2,768]{3,2,1,0:T(2,128)(2,1)S(1)}, bf16[5,32,2,768]{3,2,1,0:T(2,128)(2,1)}, u32[]{:S(2)}) copy-start(bf16[5,32,2,768]{3,2,1,0:T(2,128)(2,1)} %param.9) | copy-start | bytes 1474564
  8.8 111.5 %all-gather.9.cloned.1.call-start = ((), (), s32[]{:S(2)}) async-start(), calls=%async_computation.8 | async-start | bytes 4423680 | tf_op jit(solution)/shard_map/all_gather | solution.py:110
  10.5 14.5 %all-to-all-start.2 = ((bf16[5,32,2,768]{3,2,0,1:T(2,128)(2,1)}), bf16[5,32,2,768]{3,2,0,1:T(2,128)(2,1)S(1)}, u32[]{:S(2)}, u32[]{:S(2)}) async-start(bf16[5,32,2,768]{3,2,0,1:T(2,128)(2,1)} %copy.114), calls=%async_computation.2 | async-start | bytes 983040 | tf_op jit(solution)/shard_map/all_to_all | solution.py:114
  25.0 17.5 %all-to-all-start = ((bf16[5,32,2,768]{3,2,0,1:T(2,128)(2,1)}), bf16[5,32,2,768]{3,2,0,1:T(2,128)(2,1)S(1)}, u32[]{:S(2)}, u32[]{:S(2)}) async-start(bf16[5,32,2,768]{3,2,0,1:T(2,128)(2,1)} %copy.109), calls=%async_computation | async-start | bytes 983040 | tf_op jit(solution)/shard_map/all_to_all | solution.py:115
  43.5 29.4 %all-to-all-start.1 = ((bf16[5,64,768]{2,0,1:T(8,128)(2,1)}), bf16[5,64,768]{2,0,1:T(8,128)(2,1)S(1)}, u32[]{:S(2)}, u32[]{:S(2)}) async-start(bf16[5,64,768]{2,0,1:T(8,128)(2,1)} %bitcast.2), calls=%async_computation.1 | async-start | bytes 1572864 | tf_op jit(solution)/shard_map/all_to_all | solution.py:118
  50.8 1.1 copy-start.8
  55.3 1.8 copy-start.5
  57.1 14.6 %copy-start.11 = (f32[40,6,8]{2,1,0:T(8,128)}, f32[40,6,8]{2,1,0:T(8,128)S(1)}, u32[]{:S(2)}) copy-start(f32[40,6,8]{2,1,0:T(8,128)S(1)} %get-tuple-element.8) | copy-start | bytes 23044
  72.9 26.1 %all-to-all-start.3 = ((bf16[5,64,768]{2,0,1:T(8,128)(2,1)}), bf16[5,64,768]{2,0,1:T(8,128)(2,1)S(1)}, u32[]{:S(2)}, u32[]{:S(2)}) async-start(bf16[5,64,768]{2,0,1:T(8,128)(2,1)} %copy.121), calls=%async_computation.3 | async-start | bytes 1572864 | tf_op jit(solution)/shard_map/all_to_all | solution.py:122
  78.5 20.7 %copy-start = (bf16[8,5,8,768]{3,2,1,0:T(8,128)(2,1)}, bf16[8,5,8,768]{3,2,1,0:T(8,128)(2,1)S(1)}, u32[]{:S(2)}) copy-start(bf16[8,5,8,768]{3,2,1,0:T(8,128)(2,1)S(1)} %copy.113) | copy-start | bytes 1474564
  90.7 29.6 %copy-start.7 = (f32[768]{0:T(1024)S(1)}, f32[768]{0:T(1024)}, u32[]{:S(2)}) copy-start(f32[768]{0:T(1024)} %param.13) | copy-start | bytes 9220
  123.7 1.1 copy-start.4
  138.8 3.5 %copy-start.1 = (bf16[8,5,8,768]{3,2,1,0:T(8,128)(2,1)S(1)}, bf16[8,5,8,768]{3,2,1,0:T(8,128)(2,1)}, u32[]{:S(2)}) copy-start(bf16[8,5,8,768]{3,2,1,0:T(8,128)(2,1)} %copy-done) | copy-start | bytes 1474564
  142.6 19.7 %copy-start.6 = (bf16[768,768]{1,0:T(8,128)(2,1)S(1)}, bf16[768,768]{1,0:T(8,128)(2,1)}, u32[]{:S(2)}) copy-start(bf16[768,768]{1,0:T(8,128)(2,1)} %all-gather.7.cloned.1.call-done) | copy-start | bytes 3538948
  162.3 1.2 copy-start.9
  162.3 1.2 copy-start.12
  164.7 1.5 copy-start.10
Sparse Core Ops, SparseCore 0:
  8.9 40.0 all-gather.4
  50.5 18.4 all-gather.6
  70.6 17.4 all-gather.10
  89.5 30.7 all-gather.8
where the time goes:
time: 195 us; the launch traced here: 194 us
  waiting for transfers between devices  75.3 us (39%)
  matrix products  41.2 us (21%)
  blocking collectives  30.5 us (16%)
  starting transfers between devices  20.6 us (11%)
  between operations  13.4 us (7%)
  local copies, waits for them, and re-layouts  11.4 us (6%)
    all_gather x1, waiting for transfers between devices, per_device(): lax.all_gather(wqkv_z, 'tr', axis=0, tiled=True)  20.7 us
    all_to_all x1, blocking collectives, per_device(): lax.all_to_all(grad_columns, 'gz', split_axis=0, concat_axis=1, tiled=True)  19.6 us
    all_to_all x1, waiting for transfers between devices, per_device(): lax.all_to_all(cotangent, 'tr', split_axis=1, concat_axis=2, tiled=True)  13.1 us
    all_gather x1, waiting for transfers between devices, per_device(): lax.all_gather(wo_x, 'tr', axis=0, tiled=True)  11.9 us
    all_to_all x1, blocking collectives, per_device(): lax.all_to_all(result_lines, 'tr', split_axis=2, concat_axis=1, tiled=True)  10.9 us
    all_gather x1, waiting for transfers between devices, per_device(): lax.all_gather(wo_z, 'tr', axis=0, tiled=True)  9.53 us
    all_to_all x1, waiting for transfers between devices, per_device(): lax.all_to_all(tokens, 'tr', split_axis=1, concat_axis=2, tiled=True)  9.19 us
    all_to_all x1, waiting for transfers between devices, per_device(): lax.all_to_all(mid_lines.reshape(flat), 'gz', split_axis=1, concat_axis=0...  8.26 us
  transfers between devices with their start and end apart: 8, of which 6 were waited for; matrix products, arithmetic and copies ran while one was open for 9% of the time, Pallas kernels for 0%

commit v1 on v0

--- a/solution.py
+++ b/solution.py
@@ -1,3 +1,4 @@
+import functools
 import math
 import jax
 import jax.numpy as jnp
@@ -5,6 +6,26 @@
 from jax.sharding import PartitionSpec as P
 
 H = 6
+
+
+def measure_the_edge(z, where_dim):
+    s_next, response, outcome_arr = (lax.axis_size("tr"), lax.axis_index("tr"), z.shape[where_dim])
+    seen_now, placed = (z, 1)
+    while placed < s_next:
+        seen_now = jnp.concatenate(
+            [
+                seen_now,
+                lax.ppermute(
+                    seen_now, "tr", list(map(lambda b: (b, (b - placed) % s_next), range(s_next)))
+                ),
+            ],
+            where_dim,
+        )
+        placed = 2 * placed
+    return jnp.roll(seen_now, response * outcome_arr, where_dim)
+
+
+resolve_bars_for = functools.partial(measure_the_edge, where_dim=0)
 
 
 def head_split(packed, index, model_width):
@@ -104,7 +125,7 @@
 def per_device(tokens, cotangent, gain_x, wqkv_x, wo_x, gain_z, wqkv_z, wo_z):
     full_in_x, full_out_x = (
         lax.all_gather(wqkv_x, "tr", axis=0, tiled=True),
-        lax.all_gather(wo_x, "tr", axis=0, tiled=True),
+        resolve_bars_for(wo_x),
     )
     full_in_z, full_out_z = (
         lax.all_gather(wqkv_z, "tr", axis=0, tiled=True),

time: 195 us -> 189 us (0.969)
  waiting for transfers between devices: 75.3 us -> 58.9 us
  local copies, waits for them, and re-layouts: 11.4 us -> 18.3 us
    all_gather x1, waiting for transfers between devices: 20.7 us -> 0.44 us  [per_device(): lax.all_gather(wqkv_z, 'tr', axis=0, tiled=True)]
    all_to_all x1, waiting for transfers between devices: 13.1 us -> 28.6 us  [per_device(): lax.all_to_all(cotangent, 'tr', split_axis=1, concat_axis=2, tiled=True)]
    all_gather x1 -> x0, waiting for transfers between devices: 11.9 us -> none  [per_device(): lax.all_gather(wo_x, 'tr', axis=0, tiled=True)]
    all_gather x1, waiting for transfers between devices: 9.53 us -> 0.02 us  [per_device(): lax.all_gather(wo_z, 'tr', axis=0, tiled=True)]
    all_to_all x1, waiting for transfers between devices: 8.26 us -> 17.2 us  [per_device(): lax.all_to_all(mid_lines.reshape(flat), 'gz', split_axis=1, concat_axis=0...]
    all_to_all x1, waiting for transfers between devices: 0.01 us -> 4.43 us  [per_device(): lax.all_to_all(cot_lines.reshape(flat), 'gz', split_axis=1, concat_axis=0...]
    ppermute x0 -> x2, starting transfers between devices: none -> 4.39 us  [measure_the_edge(): lax.ppermute(seen_now, 'tr', list(map(lambda b: (b, (b - placed) % s_next...]
    unnamed x28 -> x33, local copies, waits for them, and re-layouts: 3.01 us -> 7.26 us
  transfers between devices with their start and end apart: 8 -> 9, of which waited for: 6 -> 5; matrix products, arithmetic and copies ran while one was open for 9% -> 14% of each run, Pallas kernels for 0% -> 0%
where the time goes in v1:
time: 189 us; the launch traced here: 188 us
  waiting for transfers between devices  58.9 us (31%)
  matrix products  43.1 us (23%)
  blocking collectives  30.5 us (16%)
  starting transfers between devices  21 us (11%)
  local copies, waits for them, and re-layouts  18.3 us (10%)
  between operations  13.5 us (7%)
  other arithmetic  2.79 us (1%)
    all_to_all x1, waiting for transfers between devices, per_device(): lax.all_to_all(cotangent, 'tr', split_axis=1, concat_axis=2, tiled=True)  28.6 us
    all_to_all x1, blocking collectives, per_device(): lax.all_to_all(grad_columns, 'gz', split_axis=0, concat_axis=1, tiled=True)  19.6 us
    all_to_all x1, waiting for transfers between devices, per_device(): lax.all_to_all(mid_lines.reshape(flat), 'gz', split_axis=1, concat_axis=0...  17.2 us
    all_to_all x1, blocking collectives, per_device(): lax.all_to_all(result_lines, 'tr', split_axis=2, concat_axis=1, tiled=True)  10.9 us
    unnamed x33, local copies, waits for them, and re-layouts  7.26 us
    dot_general x2, matrix products, backward(): d_normed = jnp.dot(joined, w_in.T, preferred_element_type=jnp.float32)  7.23 us
    dot_general x2, matrix products, recompute(): jnp.dot(normed, w_in, preferred_element_type=jnp.float32)  6.73 us
    dot_general x2, matrix products, backward(): jnp.einsum('bhlm,' + key_form + '->' + layout, d_scores, key_part, prefer...  6.3 us
  transfers between devices with their start and end apart: 9, of which 5 were waited for; matrix products, arithmetic and copies ran while one was open for 14% of the time, Pallas kernels for 0%

profile of v1, /device:TPU:0, one launch (start us, length us, event | category | flops | bytes accessed | tf_op | source)
XLA Modules:
  0.0 188.1 jit_solution(11789087588935349731)
XLA Ops:
  6.5 0.7 all-gather.4.cloned.1.call-update
  7.3 0.0 all-gather.8.cloned.1.call-start
  7.3 0.7 all-gather.8.cloned.1.call-update
  8.1 0.7 all-gather.6.cloned.1.call-update
  8.7 2.4 %collective-permute-start = (bf16[192,768]{1,0:T(8,128)(2,1)}, bf16[192,768]{1,0:T(8,128)(2,1)S(1)}, u32[]{:S(2)}, u32[]{:S(2)}) collective-permute-start(bf16[192,768]{1,0:T(8,128)(2,1)} %param.12), channel_id=1, source_target_pairs={{0,24},{8,0},{16,8},{24,16},{1,25},{9,1},{17,9},{25,17},{2,26},{10... | collective-permute-start | bytes 884744 | tf_op jit(solution)/shard_map/ppermute | solution.py:18
  11.2 1.1 copy.114
  12.3 3.5 %all-to-all-start.2 = ((bf16[5,32,2,768]{3,2,0,1:T(2,128)(2,1)}), bf16[5,32,2,768]{3,2,0,1:T(2,128)(2,1)S(1)}, u32[]{:S(2)}, u32[]{:S(2)}) async-start(bf16[5,32,2,768]{3,2,0,1:T(2,128)(2,1)} %copy.114), calls=%async_computation.2 | async-start | bytes 983040 | tf_op jit(solution)/shard_map/all_to_all | solution.py:135
  15.8 1.1 copy.109
  16.9 0.8 constant_dynamic-update-slice_fusion.5
  17.7 0.9 pad_maximum_fusion
  18.6 2.0 %collective-permute-start.1 = (bf16[384,768]{1,0:T(8,128)(2,1)}, bf16[384,768]{1,0:T(8,128)(2,1)}, u32[]{:S(2)}, u32[]{:S(2)}) collective-permute-start(bf16[384,768]{1,0:T(8,128)(2,1)} %pad_maximum_fusion), channel_id=1, source_target_pairs={{0,16},{8,24},{16,0},{24,8},{1,17},{9,25},{17,1},{25,9},{2,18},{10... | collective-permute-start | bytes 1769480 | tf_op jit(solution)/shard_map/ppermute | solution.py:18
  20.5 0.7 constant_dynamic-update-slice_fusion.4
  21.3 6.1 %all-to-all-done.2 = bf16[5,32,2,768]{3,2,0,1:T(2,128)(2,1)S(1)} async-done(((bf16[5,32,2,768]{3,2,0,1:T(2,128)(2,1)}), bf16[5,32,2,768]{3,2,0,1:T(2,128)(2,1)S(1)}, u32[]{:S(2)}, u32[]{:S(2)}) %all-to-all-start.2) | async-done | bytes 491552 | tf_op jit(solution)/shard_map/all_to_all | solution.py:135
  27.4 3.5 %all-to-all-start = ((bf16[5,32,2,768]{3,2,0,1:T(2,128)(2,1)}), bf16[5,32,2,768]{3,2,0,1:T(2,128)(2,1)S(1)}, u32[]{:S(2)}, u32[]{:S(2)}) async-start(bf16[5,32,2,768]{3,2,0,1:T(2,128)(2,1)} %copy.109), calls=%async_computation | async-start | bytes 983040 | tf_op jit(solution)/shard_map/all_to_all | solution.py:136
  30.9 0.6 multiply_reduce_fusion.4
  31.5 0.2 copy.178
  31.7 0.1 rsqrt.24
  31.8 0.7 copy.119
  32.5 28.6 %all-to-all-done = bf16[5,32,2,768]{3,2,0,1:T(2,128)(2,1)S(1)} async-done(((bf16[5,32,2,768]{3,2,0,1:T(2,128)(2,1)}), bf16[5,32,2,768]{3,2,0,1:T(2,128)(2,1)S(1)}, u32[]{:S(2)}, u32[]{:S(2)}) %all-to-all-start) | async-done | bytes 491552 | tf_op jit(solution)/shard_map/all_to_all | solution.py:136
  61.1 1.0 copy.144
  62.1 5.8 %all-to-all-start.1 = ((bf16[5,64,768]{2,0,1:T(8,128)(2,1)}), bf16[5,64,768]{2,0,1:T(8,128)(2,1)S(1)}, u32[]{:S(2)}, u32[]{:S(2)}) async-start(bf16[5,64,768]{2,0,1:T(8,128)(2,1)} %bitcast.2), calls=%async_computation.1 | async-start | bytes 1572864 | tf_op jit(solution)/shard_map/all_to_all | solution.py:139
  68.0 0.4 copy_bitcast_fusion
  68.4 0.7 reshape.140
  69.0 1.9 %constant_dynamic-update-slice_fusion.3 = bf16[1536,768]{1,0:T(8,128)(2,1)} fusion(bf16[1536,768]{1,0:T(8,128)(2,1)} %constant_dynamic-update-slice_fusion.4, bf16[384,768]{1,0:T(8,128)(2,1)} %collective-permute-done.1), kind=kLoop, calls=%fused_computation.111 | loop fusion | bytes 1179648
  71.0 0.8 constant_dynamic-update-slice_fusion.2
  71.8 0.8 constant_dynamic-update-slice_fusion.1
  72.5 2.0 %constant_dynamic-update-slice_fusion = bf16[1536,768]{1,0:T(8,128)(2,1)} fusion(bf16[1536,768]{1,0:T(8,128)(2,1)} %constant_dynamic-update-slice_fusion.1, bf16[384,768]{1,0:T(8,128)(2,1)} %collective-permute-done.1), kind=kLoop, calls=%fused_computation.108 | loop fusion | bytes 1179648 | tf_op jit(solution)/shard_map/jit(_roll_dynamic)/concatenate | solution.py:25
  74.5 3.4 %convolution_convert_fusion.1 = bf16[40,8,2304]{2,1,0:T(8,128)(2,1)S(1)} fusion(bf16[768,2304]{1,0:T(8,128)(2,1)} %all-gather.4.cloned.1.call-done, f32[40,8,768]{2,1,0:T(8,128)S(1)} %reshape.140, f32[768]{0:T(1024)S(1)} %copy-done.11, f32[40,8]{1,0:T(8,128)} %copy.119), kind=kOutput, calls=%fused_computation.5 | convolution fusion | flops 1133936640 | bytes 6000896 | tf_op jit(solution)/shard_map/dot_general | solution.py:46
  77.9 1.8 fusion.109
  79.7 2.7 %fusion.40 = bf16[40,8,768]{2,1,0:T(8,128)(2,1)S(1)} fusion(f32[40,8,768]{2,1,0:T(8,128)S(1)} %reshape.140, bf16[1536,768]{1,0:T(8,128)(2,1)} %constant_dynamic-update-slice_fusion, s32[]{:T(128)S(6)} %select_n.14, bf16[40,8,2304]{2,1,0:T(8,128)(2,1)} %copy-done.8, f32[40,6,8,8]{2,3,1,0:T(8,128)} %get-tuple-element.9, f32[40,6,8]{2,1,0:T(8,128)S(1)} %get-tuple-element.8), kind=kOutput, calls=%fused_computation.38 | convolution fusion | flops 382187520 | bytes 4136452 | tf_op jit(solution)/shard_map/dot_general | solution.py:75
  82.4 1.2 copy.121
  83.6 4.4 %all-to-all-done.1 = bf16[5,64,768]{2,0,1:T(8,128)(2,1)S(1)} async-done(((bf16[5,64,768]{2,0,1:T(8,128)(2,1)}), bf16[5,64,768]{2,0,1:T(8,128)(2,1)S(1)}, u32[]{:S(2)}, u32[]{:S(2)}) %all-to-all-start.1) | async-done | bytes 491552 | tf_op jit(solution)/shard_map/all_to_all | solution.py:139
  88.0 3.7 %all-to-all-start.3 = ((bf16[5,64,768]{2,0,1:T(8,128)(2,1)}), bf16[5,64,768]{2,0,1:T(8,128)(2,1)S(1)}, u32[]{:S(2)}, u32[]{:S(2)}) async-start(bf16[5,64,768]{2,0,1:T(8,128)(2,1)} %copy.121), calls=%async_computation.3 | async-start | bytes 1572864 | tf_op jit(solution)/shard_map/all_to_all | solution.py:143
  91.7 0.1 copy.113
  91.9 2.8 %fusion.43 = bf16[40,8,6,128]{3,1,2,0:T(8,128)(2,1)} fusion(bf16[40,8,768]{2,1,0:T(8,128)(2,1)S(1)} %bitcast.138, bf16[768,768]{1,0:T(8,128)(2,1)} %all-gather.8.cloned.1.call-done), kind=kOutput, calls=%fused_computation.50 | convolution fusion | flops 377733120 | bytes 2162688 | tf_op jit(solution)/shard_map/dot_general | solution.py:85
  94.7 17.2 %all-to-all-done.3 = bf16[5,64,768]{2,0,1:T(8,128)(2,1)S(1)} async-done(((bf16[5,64,768]{2,0,1:T(8,128)(2,1)}), bf16[5,64,768]{2,0,1:T(8,128)(2,1)S(1)}, u32[]{:S(2)}, u32[]{:S(2)}) %all-to-all-start.3) | async-done | bytes 491552 | tf_op jit(solution)/shard_map/all_to_all | solution.py:143
  111.9 0.3 multiply_reduce_fusion
  112.2 0.1 copy.122
  112.2 0.1 reshape.151
  112.4 0.1 copy.125
  112.5 0.4 all-gather.6.cloned.1.call-done
  112.9 3.3 %convolution_convert_fusion = bf16[40,8,2304]{2,1,0:T(8,128)(2,1)S(1)} fusion(bf16[768,2304]{1,0:T(8,128)(2,1)} %all-gather.6.cloned.1.call-done, f32[40,8,768]{2,1,0:T(8,128)S(1)} %bitcast.135, f32[768]{0:T(1024)S(1)} %copy-done.10, f32[40,8]{1,0:T(8,128)S(1)} %reshape.158), kind=kOutput, calls=%fused_computation.4 | convolution fusion | flops 1133936640 | bytes 6000896 | tf_op jit(solution)/shard_map/dot_general | solution.py:46
  116.3 1.1 slice_bitcast_fusion
  117.3 0.0 copy-done.7
  117.4 0.4 fusion.62
  117.8 2.8 %fusion.110 = (f32[8,6,40]{2,1,0:T(8,128)S(1)}, f32[8,6,40,40]{2,3,1,0:T(8,128)}) fusion(bf16[40,8,6,128]{3,1,2,0:T(8,128)(2,1)} %get-tuple-element.7, bf16[40,8,6,128]{3,1,2,0:T(8,128)(2,1)} %get-tuple-element.6), kind=kOutput, calls=%fused_computation.134 | convolution fusion | flops 19891240 | bytes 1297920 | tf_op jit(solution)/shard_map/sub | solution.py:61
  120.6 2.6 %fusion.48 = bf16[40,8,6,128]{3,0,2,1:T(8,128)(2,1)} fusion(bf16[40,8,6,128]{3,1,2,0:T(8,128)(2,1)} %fusion.43, f32[8,6,40,40]{2,3,1,0:T(8,128)} %get-tuple-element.11, f32[8,6,40]{2,1,0:T(8,128)S(1)} %get-tuple-element.10), kind=kOutput, calls=%fused_computation.55 | convolution fusion | flops 20060160 | bytes 1297920 | tf_op jit(solution)/shard_map/bhlm,lbhe->mbhe/dot_general | solution.py:90
  123.1 3.0 %fusion.47 = bf16[40,8,6,128]{3,0,2,1:T(8,128)(2,1)} fusion(f32[8,6,40,40]{2,3,1,0:T(8,128)S(1)} %fusion.62, bf16[40,8,6,128]{3,1,2,0:T(8,128)(2,1)} %get-tuple-element.6, f32[8,6,40,40]{2,3,1,0:T(8,128)} %get-tuple-element.11, f32[8,6,40]{2,1,0:T(8,128)S(1)} %get-tuple-element.10), kind=kOutput, calls=%fused_computation.54 | convolution fusion | flops 20446120 | bytes 1605120 | tf_op jit(solution)/shard_map/bhlm,lbhe->mbhe/dot_general | solution.py:98
  126.1 3.1 %fusion.46 = bf16[40,8,6,128]{3,0,2,1:T(8,128)(2,1)} fusion(f32[8,6,40,40]{2,3,1,0:T(8,128)S(1)} %fusion.62, bf16[40,8,6,128]{3,1,2,0:T(8,128)(2,1)} %get-tuple-element.7, f32[8,6,40,40]{2,3,1,0:T(8,128)} %get-tuple-element.11, f32[8,6,40]{2,1,0:T(8,128)S(1)} %get-tuple-element.10), kind=kOutput, calls=%fused_computation.53 | convolution fusion | flops 20446120 | bytes 1605120 | tf_op jit(solution)/shard_map/bhlm,mbhe->lbhe/dot_general | solution.py:95
  129.2 1.2 copy.183
  130.3 1.4 copy_bitcast_fusion.1
  131.7 3.5 %multiply_reduce_fusion.3 = (f32[40,8]{1,0:T(8,128)S(1)}, f32[40,8,768]{2,1,0:T(8,128)S(1)}) fusion(f32[40,8,768]{2,1,0:T(8,128)S(1)} %bitcast.136, f32[768]{0:T(1024)S(1)} %copy-done.10, bf16[768,2304]{1,0:T(8,128)(2,1)} %all-gather.6.cloned.1.call-done, bf16[40,8,768]{2,1,0:T(8,128)(2,1)S(1)} %get-tuple-element.16, ...), kind=kOutput, calls=%fused_computation.71 | convolution fusion | flops 1137622784 | bytes 6983936 | tf_op jit(solution)/shard_map/dot_general | solution.py:104
  135.2 0.3 add_convert_fusion.1
  135.5 19.6 %all_to_all.84 = bf16[40,8,768]{2,1,0:T(8,128)(2,1)S(1)} all-to-all(bf16[40,8,768]{2,1,0:T(8,128)(2,1)S(1)} %add_convert_fusion.1), channel_id=1, replica_groups=mesh['tr'=4,'gz'=8] {'gz'}, dimensions={0} | all-to-all | bytes 983040 | tf_op jit(solution)/shard_map/all_to_all | solution.py:147
  155.2 1.9 fusion.44
  157.1 0.4 fusion.51
  157.5 1.4 fusion.81
  158.9 3.2 %fusion.49 = bf16[40,8,768]{2,1,0:T(8,128)(2,1)} fusion(f32[40,6,8,8]{2,3,1,0:T(8,128)S(1)} %fusion.81, bf16[40,8,2304]{2,1,0:T(8,128)(2,1)} %copy-done.8, f32[40,6,8,8]{2,3,1,0:T(8,128)} %get-tuple-element.9, f32[40,6,8]{2,1,0:T(8,128)S(1)} %get-tuple-element.8), kind=kOutput, calls=%fused_computation.56 | convolution fusion | flops 4287367 | bytes 4321280 | tf_op jit(solution)/shard_map/bhlm,bmhe->blhe/dot_general | solution.py:95
  162.2 3.2 %fusion.50 = bf16[40,8,768]{2,1,0:T(8,128)(2,1)} fusion(f32[40,6,8,8]{2,3,1,0:T(8,128)S(1)} %fusion.81, bf16[40,8,2304]{2,1,0:T(8,128)(2,1)} %copy-done.8, f32[40,6,8,8]{2,3,1,0:T(8,128)} %get-tuple-element.9, f32[40,6,8]{2,1,0:T(8,128)S(1)} %get-tuple-element.8), kind=kOutput, calls=%fused_computation.57 | convolution fusion | flops 4287367 | bytes 4321280 | tf_op jit(solution)/shard_map/bhlm,blhe->bmhe/dot_general | solution.py:98
  165.4 3.7 %multiply_reduce_fusion.2 = (f32[40,8]{1,0:T(8,128)S(1)}, f32[40,8,768]{2,1,0:T(8,128)S(1)}) fusion(f32[40,8,768]{2,1,0:T(8,128)S(1)} %reshape.140, f32[768]{0:T(1024)S(1)} %copy-done.11, bf16[768,2304]{1,0:T(8,128)(2,1)} %all-gather.4.cloned.1.call-done, bf16[40,8,768]{2,1,0:T(8,128)(2,1)S(1)} %fusion.51, bf16[40,8,768]{2,1,0:T(8,128)(2,1)} %fusion.50, ...), kind=kOutput, calls=%fused_computation.69 | convolution fusion | flops 1137622784 | bytes 6983936 | tf_op jit(solution)/shard_map/dot_general | solution.py:104
  169.1 0.3 add_convert_fusion
  169.5 0.1 copy.139
  169.6 10.9 %all_to_all.85 = bf16[5,8,8,768]{3,1,0,2:T(8,128)(2,1)S(1)} all-to-all(bf16[5,8,8,768]{3,1,0,2:T(8,128)(2,1)S(1)} %copy.139), channel_id=1, replica_groups=mesh['tr'=4,'gz'=8] {'tr'}, dimensions={2} | all-to-all | bytes 983040 | tf_op jit(solution)/shard_map/all_to_all | solution.py:151
  180.4 1.2 copy.140
  (39 shorter events, 0.2 us)
Async XLA Ops:
  6.5 10.4 %copy-start = (bf16[192,768]{1,0:T(8,128)(2,1)S(1)}, bf16[192,768]{1,0:T(8,128)(2,1)}, u32[]{:S(2)}) copy-start(bf16[192,768]{1,0:T(8,128)(2,1)} %param.12) | copy-start | bytes 884740
  6.5 4.6 %copy-start.5 = (bf16[5,32,2,768]{3,2,1,0:T(2,128)(2,1)S(1)}, bf16[5,32,2,768]{3,2,1,0:T(2,128)(2,1)}, u32[]{:S(2)}) copy-start(bf16[5,32,2,768]{3,2,1,0:T(2,128)(2,1)} %param.8) | copy-start | bytes 1474564
  6.5 9.3 %copy-start.6 = (bf16[5,32,2,768]{3,2,1,0:T(2,128)(2,1)S(1)}, bf16[5,32,2,768]{3,2,1,0:T(2,128)(2,1)}, u32[]{:S(2)}) copy-start(bf16[5,32,2,768]{3,2,1,0:T(2,128)(2,1)} %param.9) | copy-start | bytes 1474564
  6.5 68.0 %all-gather.4.cloned.1.call-start = ((), (), s32[]{:S(2)}) async-start(), calls=%async_computation.6 | async-start | bytes 4423680 | tf_op jit(solution)/shard_map/all_gather | solution.py:127
  7.3 84.6 %all-gather.8.cloned.1.call-start = ((), (), s32[]{:S(2)}) async-start(), calls=%async_computation.8 | async-start | bytes 1474560 | tf_op jit(solution)/shard_map/all_gather | solution.py:132
  8.0 104.9 %all-gather.6.cloned.1.call-start = ((), (), s32[]{:S(2)}) async-start(), calls=%async_computation.7 | async-start | bytes 4423680 | tf_op jit(solution)/shard_map/all_gather | solution.py:131
  8.7 8.9 %collective-permute-start = (bf16[192,768]{1,0:T(8,128)(2,1)}, bf16[192,768]{1,0:T(8,128)(2,1)S(1)}, u32[]{:S(2)}, u32[]{:S(2)}) collective-permute-start(bf16[192,768]{1,0:T(8,128)(2,1)} %param.12), channel_id=1, source_target_pairs={{0,24},{8,0},{16,8},{24,16},{1,25},{9,1},{17,9},{25,17},{2,26},{10... | collective-permute-start | bytes 884744 | tf_op jit(solution)/shard_map/ppermute | solution.py:18
  12.3 15.1 %all-to-all-start.2 = ((bf16[5,32,2,768]{3,2,0,1:T(2,128)(2,1)}), bf16[5,32,2,768]{3,2,0,1:T(2,128)(2,1)S(1)}, u32[]{:S(2)}, u32[]{:S(2)}) async-start(bf16[5,32,2,768]{3,2,0,1:T(2,128)(2,1)} %copy.114), calls=%async_computation.2 | async-start | bytes 983040 | tf_op jit(solution)/shard_map/all_to_all | solution.py:135
  17.7 44.5 %copy-start.1 = (bf16[192,768]{1,0:T(8,128)(2,1)}, bf16[192,768]{1,0:T(8,128)(2,1)S(1)}, u32[]{:S(2)}) copy-start(bf16[192,768]{1,0:T(8,128)(2,1)S(1)} %collective-permute-done) | copy-start | bytes 884740
  18.6 50.5 %collective-permute-start.1 = (bf16[384,768]{1,0:T(8,128)(2,1)}, bf16[384,768]{1,0:T(8,128)(2,1)}, u32[]{:S(2)}, u32[]{:S(2)}) collective-permute-start(bf16[384,768]{1,0:T(8,128)(2,1)} %pad_maximum_fusion), channel_id=1, source_target_pairs={{0,16},{8,24},{16,0},{24,8},{1,17},{9,25},{17,1},{25,9},{2,18},{10... | collective-permute-start | bytes 1769480 | tf_op jit(solution)/shard_map/ppermute | solution.py:18
  27.4 33.7 %all-to-all-start = ((bf16[5,32,2,768]{3,2,0,1:T(2,128)(2,1)}), bf16[5,32,2,768]{3,2,0,1:T(2,128)(2,1)S(1)}, u32[]{:S(2)}, u32[]{:S(2)}) async-start(bf16[5,32,2,768]{3,2,0,1:T(2,128)(2,1)} %copy.109), calls=%async_computation | async-start | bytes 983040 | tf_op jit(solution)/shard_map/all_to_all | solution.py:136
  62.1 25.9 %all-to-all-start.1 = ((bf16[5,64,768]{2,0,1:T(8,128)(2,1)}), bf16[5,64,768]{2,0,1:T(8,128)(2,1)S(1)}, u32[]{:S(2)}, u32[]{:S(2)}) async-start(bf16[5,64,768]{2,0,1:T(8,128)(2,1)} %bitcast.2), calls=%async_computation.1 | async-start | bytes 1572864 | tf_op jit(solution)/shard_map/all_to_all | solution.py:139
  68.3 3.4 %copy-start.2 = (bf16[192,768]{1,0:T(8,128)(2,1)S(1)}, bf16[192,768]{1,0:T(8,128)(2,1)}, u32[]{:S(2)}) copy-start(bf16[192,768]{1,0:T(8,128)(2,1)} %copy-done.1) | copy-start | bytes 884740
  68.3 6.2 %copy-start.11 = (f32[768]{0:T(1024)S(1)}, f32[768]{0:T(1024)}, u32[]{:S(2)}) copy-start(f32[768]{0:T(1024)} %param.10) | copy-start | bytes 9220
  77.9 1.8 copy-start.8
  88.0 23.9 %all-to-all-start.3 = ((bf16[5,64,768]{2,0,1:T(8,128)(2,1)}), bf16[5,64,768]{2,0,1:T(8,128)(2,1)S(1)}, u32[]{:S(2)}, u32[]{:S(2)}) async-start(bf16[5,64,768]{2,0,1:T(8,128)(2,1)} %copy.121), calls=%async_computation.3 | async-start | bytes 1572864 | tf_op jit(solution)/shard_map/all_to_all | solution.py:143
  91.9 20.5 %copy-start.3 = (bf16[8,5,8,768]{3,2,1,0:T(8,128)(2,1)}, bf16[8,5,8,768]{3,2,1,0:T(8,128)(2,1)S(1)}, u32[]{:S(2)}) copy-start(bf16[8,5,8,768]{3,2,1,0:T(8,128)(2,1)S(1)} %copy.113) | copy-start | bytes 1474564
  91.9 21.0 %copy-start.10 = (f32[768]{0:T(1024)S(1)}, f32[768]{0:T(1024)}, u32[]{:S(2)}) copy-start(f32[768]{0:T(1024)} %param.13) | copy-start | bytes 9220
  116.3 1.1 copy-start.7
  131.7 3.5 %copy-start.4 = (bf16[8,5,8,768]{3,2,1,0:T(8,128)(2,1)S(1)}, bf16[8,5,8,768]{3,2,1,0:T(8,128)(2,1)}, u32[]{:S(2)}) copy-start(bf16[8,5,8,768]{3,2,1,0:T(8,128)(2,1)} %copy-done.3) | copy-start | bytes 1474564
  135.5 21.6 %copy-start.12 = (f32[40,6,8,8]{2,3,1,0:T(8,128)S(1)}, f32[40,6,8,8]{2,3,1,0:T(8,128)}, u32[]{:S(2)}) copy-start(f32[40,6,8,8]{2,3,1,0:T(8,128)} %get-tuple-element.9) | copy-start | bytes 184324
  165.4 3.8 %copy-start.9 = (f32[40,8]{1,0:T(8,128)S(1)}, f32[40,8]{1,0:T(8,128)}, u32[]{:S(2)}) copy-start(f32[40,8]{1,0:T(8,128)} %copy.119) | copy-start | bytes 3844
Sparse Core Ops, SparseCore 0:
  8.9 52.5 all-gather.3
  63.1 17.4 all-gather.7
  82.1 30.7 all-gather.5
